TPU v7x, 32 devices: a whole 2x2x4 slice. The times are simulated.
32 devices in a mesh: seq: 4 (over y, x), shard: 8 (over z, core).
Axes of the slice: x: 2, y: 2, z: 4, core: 2. Of those that a mesh axis runs over, the one named last changes fastest.
Arguments:
- hidden_in: bfloat16 [16, 2048, 768], P('shard', 'seq'), may hold values from -6 to 6
- seq_lengths: int32 [16], P('shard'), may hold values from 1 to 2048, as said below
- w_qkv: bfloat16 [768, 2304], P('shard'), may hold values from -0.21875 to 0.21875
- b_query: bfloat16 [768], P('shard'), may hold values from -1.5 to 1.5
- b_value: bfloat16 [768], P('shard'), may hold values from -0.5 to 0.5
- w_out: bfloat16 [768, 768], P('shard'), may hold values from -6 to 6
- b_out: bfloat16 [768], P('shard'), may hold values from -1 to 1
- ln1_gain: bfloat16 [768], P('shard'), may hold values from 0.5 to 1.5
- ln1_bias: bfloat16 [768], P('shard'), may hold values from -1 to 1
- w_up: bfloat16 [768, 3072], P('shard'), may hold values from -0.21875 to 0.21875
- b_up: bfloat16 [3072], P('shard'), may hold values from -1 to 1
- w_down: bfloat16 [3072, 768], P('shard'), may hold values from -0.109375 to 0.109375
- b_down: bfloat16 [768], P('shard'), may hold values from -1 to 1
- ln2_gain: bfloat16 [768], P('shard'), may hold values from 0.5 to 1.5
- ln2_bias: bfloat16 [768], P('shard'), may hold values from -1 to 1
- cotangent: bfloat16 [16, 2048, 768], P('shard', 'seq'), may hold values from -6 to 6
Outputs:
- output: bfloat16 [16, 2048, 768], P('shard', 'seq')
- grad_input: bfloat16 [16, 2048, 768], P('shard', 'seq')
- grad_w_qkv: float32 [768, 2304], P('shard')
- grad_b_query: float32 [768], P('shard')
- grad_b_value: float32 [768], P('shard')
- grad_w_out: float32 [768, 768], P('shard')
- grad_b_out: float32 [768], P('shard')
- grad_ln1_gain: float32 [768], P('shard')
- grad_ln1_bias: float32 [768], P('shard')
- grad_w_up: float32 [768, 3072], P('shard')
- grad_b_up: float32 [3072], P('shard')
- grad_w_down: float32 [3072, 768], P('shard')
- grad_b_down: float32 [768], P('shard')
- grad_ln2_gain: float32 [768], P('shard')
- grad_ln2_bias: float32 [768], P('shard')
Inputs may be any that keep to these rules, and one draw needn't show every extreme that they name: `seq_lengths`: of sequences 2 i and 2 i + 1, at least one has all 2048 positions valid.
All inputs are finite; a program needn't handle non-finite values.
Results may differ from a plain program's by a relative error of at most 0.018.
Values may be sent and summed in bfloat16 or wider, within the bound.
A program may use at most 192 MiB of HBM per device.

v0:
```python
import jax
import jax.numpy as jnp
from jax import lax
from jax.sharding import PartitionSpec as P

DH = 64
EPS = 1e-12
NEG_FILL = -1e30
HALF_ROOT = 0.7071067811865476
INV_ROOT_TAU = 0.3989422804014327


def dot_rows(left_op, right_op):
    return lax.dot_general(
        left_op, right_op, (((0,), (0,)), ((), ())), preferred_element_type=jnp.float32
    )


def dot_last(left_op, right_op):
    return lax.dot_general(
        left_op, right_op, (((1,), (1,)), ((), ())), preferred_element_type=jnp.float32
    )


def owner_order(grad_arr, shard_count, group_count):
    rows = grad_arr.shape[0]
    piece = rows // (shard_count * group_count)
    rest = grad_arr.shape[1:]
    split = grad_arr.reshape((shard_count, group_count, piece) + rest)
    return jnp.swapaxes(split, 0, 1).reshape(grad_arr.shape)


def reorder_all(grad_list, shard_count, group_count):
    return tuple((owner_order(grad_arr, shard_count, group_count) for grad_arr in grad_list))


def norm_forward(hidden, gain_vec, shift_vec):
    mean_val = jnp.mean(hidden, axis=-1, keepdims=True)
    centered = hidden - mean_val
    inv_std = lax.rsqrt(jnp.mean(centered * centered, axis=-1, keepdims=True) + EPS)
    normed = centered * inv_std
    return (normed * gain_vec + shift_vec, normed, inv_std)


def norm_backward(grad_out, normed, inv_std, gain_vec):
    grad_gain = jnp.sum(grad_out * normed, axis=0)
    grad_shift = jnp.sum(grad_out, axis=0)
    scaled = grad_out * gain_vec
    grad_in = inv_std * (
        scaled
        - jnp.mean(scaled, axis=-1, keepdims=True)
        - normed * jnp.mean(scaled * normed, axis=-1, keepdims=True)
    )
    return (grad_in, grad_gain, grad_shift)


def gelu_parts(pre_act):
    cdf_val = 0.5 * (1.0 + lax.erf(pre_act * HALF_ROOT))
    pdf_val = jnp.exp(-0.5 * pre_act * pre_act) * INV_ROOT_TAU
    return (pre_act * cdf_val, cdf_val + pre_act * pdf_val)


def masked_scores(query_blk, keys_all, key_valid, scale_val):
    scores = (
        jnp.einsum("bhd,khd->hbk", query_blk, keys_all, preferred_element_type=jnp.float32)
        * scale_val
    )
    return jnp.where(key_valid[None, None, :], scores, NEG_FILL)


def attend_forward(head_data, length, block_rows):
    seq_len = head_data.shape[0]
    heads_here = head_data.shape[2]
    head_size = head_data.shape[3]
    keys_all = head_data[:, 1]
    values_all = head_data[:, 2]
    key_valid = jnp.arange(seq_len) < length
    scale_val = head_size ** (-0.5)
    query_blocks = head_data[:, 0].reshape(seq_len // block_rows, block_rows, heads_here, head_size)

    def one_block(query_blk):
        scores = masked_scores(query_blk, keys_all, key_valid, scale_val)
        row_max = jnp.max(scores, axis=-1, keepdims=True)
        exp_scores = jnp.exp(scores - row_max)
        row_sum = jnp.sum(exp_scores, axis=-1, keepdims=True)
        attn_prob = (exp_scores / row_sum).astype(jnp.bfloat16)
        out_blk = jnp.einsum(
            "hbk,khd->bhd", attn_prob, values_all, preferred_element_type=jnp.float32
        )
        return (out_blk, (row_max + jnp.log(row_sum))[..., 0])

    out_blocks, row_lse = lax.map(one_block, query_blocks)
    return (out_blocks.reshape(seq_len, heads_here, head_size), row_lse)


def attend_backward(head_data, grad_att, row_lse, length, block_rows):
    seq_len = head_data.shape[0]
    heads_here = head_data.shape[2]
    head_size = head_data.shape[3]
    keys_all = head_data[:, 1]
    values_all = head_data[:, 2]
    key_valid = jnp.arange(seq_len) < length
    scale_val = head_size ** (-0.5)
    block_count = seq_len // block_rows
    query_blocks = head_data[:, 0].reshape(block_count, block_rows, heads_here, head_size)
    grad_blocks = grad_att.reshape(block_count, block_rows, heads_here, head_size)

    def one_block(carried, pieces):
        grad_keys, grad_values = carried
        query_blk, grad_blk, lse_blk = pieces
        scores = masked_scores(query_blk, keys_all, key_valid, scale_val)
        attn_prob = jnp.exp(scores - lse_blk[..., None])
        grad_prob = jnp.einsum(
            "bhd,khd->hbk", grad_blk, values_all, preferred_element_type=jnp.float32
        )
        row_dot = jnp.sum(grad_prob * attn_prob, axis=-1, keepdims=True)
        grad_scores = (attn_prob * (grad_prob - row_dot)).astype(jnp.bfloat16)
        grad_query = (
            jnp.einsum("hbk,khd->bhd", grad_scores, keys_all, preferred_element_type=jnp.float32)
            * scale_val
        )
        grad_keys = (
            grad_keys
            + jnp.einsum("hbk,bhd->khd", grad_scores, query_blk, preferred_element_type=jnp.float32)
            * scale_val
        )
        grad_values = grad_values + jnp.einsum(
            "hbk,bhd->khd",
            attn_prob.astype(jnp.bfloat16),
            grad_blk,
            preferred_element_type=jnp.float32,
        )
        return ((grad_keys, grad_values), grad_query)

    zeros_kv = jnp.zeros((seq_len, heads_here, head_size), jnp.float32)
    (grad_keys, grad_values), grad_queries = lax.scan(
        one_block, (zeros_kv, zeros_kv), (query_blocks, grad_blocks, row_lse)
    )
    grad_queries = grad_queries.reshape(seq_len, heads_here, head_size)
    return jnp.stack([grad_queries, grad_keys, grad_values], axis=1).astype(jnp.bfloat16)


def per_device(
    hidden_in,
    seq_lengths,
    w_qkv,
    b_query,
    b_value,
    w_out,
    b_out,
    ln1_gain,
    ln1_bias,
    w_up,
    b_up,
    w_down,
    b_down,
    ln2_gain,
    ln2_bias,
    cotangent,
):
    group_count = lax.axis_size("seq")
    shard_count = lax.axis_size("shard")
    seq_count = hidden_in.shape[0]
    pos_count = hidden_in.shape[1]
    model_width = hidden_in.shape[2]
    tok_count = seq_count * pos_count
    full_len = pos_count * group_count
    group_width = model_width // group_count
    heads_here = group_width // DH
    block_rows = min(512, full_len)
    gathered = (
        lax.all_gather(w_qkv, "shard", axis=0, tiled=True),
        lax.all_gather(b_query, "shard", axis=0, tiled=True),
        lax.all_gather(b_value, "shard", axis=0, tiled=True),
        lax.all_gather(w_out, "shard", axis=0, tiled=True),
        lax.all_gather(b_out, "shard", axis=0, tiled=True),
        lax.all_gather(ln1_gain, "shard", axis=0, tiled=True),
        lax.all_gather(ln1_bias, "shard", axis=0, tiled=True),
        lax.all_gather(w_up, "shard", axis=0, tiled=True),
        lax.all_gather(b_up, "shard", axis=0, tiled=True),
        lax.all_gather(w_down, "shard", axis=0, tiled=True),
        lax.all_gather(b_down, "shard", axis=0, tiled=True),
        lax.all_gather(ln2_gain, "shard", axis=0, tiled=True),
        lax.all_gather(ln2_bias, "shard", axis=0, tiled=True),
    )
    (
        qkv_weight,
        query_bias,
        value_bias,
        out_weight,
        out_bias,
        gain_one,
        shift_one,
        up_weight,
        up_bias,
        down_weight,
        down_bias,
        gain_two,
        shift_two,
    ) = gathered
    gain_one = gain_one.astype(jnp.float32)
    gain_two = gain_two.astype(jnp.float32)
    tokens = hidden_in.reshape(tok_count, model_width)
    qkv_bias = jnp.concatenate([query_bias, jnp.zeros_like(query_bias), value_bias]).astype(
        jnp.float32
    )
    qkv_tok = (jnp.dot(tokens, qkv_weight, preferred_element_type=jnp.float32) + qkv_bias).astype(
        jnp.bfloat16
    )
    head_data = lax.all_to_all(
        qkv_tok.reshape(seq_count, pos_count, 3, group_count, group_width),
        "seq",
        split_axis=3,
        concat_axis=1,
        tiled=True,
    )
    head_data = head_data.reshape(seq_count, full_len, 3, heads_here, DH)
    attended_list = []
    lse_list = []
    for seq_pos in range(seq_count):
        out_seq, lse_seq = attend_forward(head_data[seq_pos], seq_lengths[seq_pos], block_rows)
        attended_list.append(out_seq)
        lse_list.append(lse_seq)
    attended_heads = (
        jnp.stack(attended_list).astype(jnp.bfloat16).reshape(seq_count, full_len, 1, group_width)
    )
    attended = lax.all_to_all(
        attended_heads, "seq", split_axis=1, concat_axis=2, tiled=True
    ).reshape(tok_count, model_width)
    projected = jnp.dot(attended, out_weight, preferred_element_type=jnp.float32) + out_bias.astype(
        jnp.float32
    )
    ln_one, normed_one, inv_one = norm_forward(
        tokens.astype(jnp.float32) + projected, gain_one, shift_one.astype(jnp.float32)
    )
    ln_low = ln_one.astype(jnp.bfloat16)
    pre_act = jnp.dot(ln_low, up_weight, preferred_element_type=jnp.float32) + up_bias.astype(
        jnp.float32
    )
    act_val, act_slope = gelu_parts(pre_act)
    act_low = act_val.astype(jnp.bfloat16)
    ffn_out = jnp.dot(act_low, down_weight, preferred_element_type=jnp.float32) + down_bias.astype(
        jnp.float32
    )
    result, normed_two, inv_two = norm_forward(
        ln_one + ffn_out, gain_two, shift_two.astype(jnp.float32)
    )
    output = result.astype(jnp.bfloat16).reshape(seq_count, pos_count, model_width)
    grad_y = cotangent.reshape(tok_count, model_width).astype(jnp.float32)
    grad_two, grad_gain_two, grad_shift_two = norm_backward(grad_y, normed_two, inv_two, gain_two)
    grad_ffn = grad_two.astype(jnp.bfloat16)
    grad_down_bias = jnp.sum(grad_ffn, axis=0, dtype=jnp.float32)
    grad_down_weight = dot_rows(act_low, grad_ffn)
    grad_pre = (dot_last(grad_ffn, down_weight) * act_slope).astype(jnp.bfloat16)
    grad_up_bias = jnp.sum(grad_pre, axis=0, dtype=jnp.float32)
    grad_up_weight = dot_rows(ln_low, grad_pre)
    grad_ln = dot_last(grad_pre, up_weight) + grad_two
    grad_one, grad_gain_one, grad_shift_one = norm_backward(grad_ln, normed_one, inv_one, gain_one)
    grad_proj = grad_one.astype(jnp.bfloat16)
    grad_out_bias = jnp.sum(grad_proj, axis=0, dtype=jnp.float32)
    grad_out_weight = dot_rows(attended, grad_proj)
    grad_att = dot_last(grad_proj, out_weight).astype(jnp.bfloat16)
    grad_heads = lax.all_to_all(
        grad_att.reshape(seq_count, pos_count, group_count, group_width),
        "seq",
        split_axis=2,
        concat_axis=1,
        tiled=True,
    )
    grad_heads = grad_heads.reshape(seq_count, full_len, heads_here, DH)
    grad_list = []
    for seq_pos in range(seq_count):
        grad_list.append(
            attend_backward(
                head_data[seq_pos],
                grad_heads[seq_pos],
                lse_list[seq_pos],
                seq_lengths[seq_pos],
                block_rows,
            )
        )
    grad_qkv_heads = jnp.stack(grad_list).reshape(seq_count, full_len, 3, 1, group_width)
    grad_qkv = lax.all_to_all(
        grad_qkv_heads, "seq", split_axis=1, concat_axis=3, tiled=True
    ).reshape(tok_count, 3 * model_width)
    grad_qkv_weight = dot_rows(tokens, grad_qkv)
    grad_query_bias = jnp.sum(grad_qkv[:, :model_width], axis=0, dtype=jnp.float32)
    grad_value_bias = jnp.sum(grad_qkv[:, 2 * model_width :], axis=0, dtype=jnp.float32)
    grad_input = (
        (dot_last(grad_qkv, qkv_weight) + grad_one)
        .astype(jnp.bfloat16)
        .reshape(seq_count, pos_count, model_width)
    )
    attn_list = (
        grad_qkv_weight,
        grad_query_bias,
        grad_value_bias,
        grad_out_weight,
        grad_out_bias,
        grad_gain_one,
        grad_shift_one,
    )
    every_grad = attn_list + (
        grad_up_weight,
        grad_up_bias,
        grad_down_weight,
        grad_down_bias,
        grad_gain_two,
        grad_shift_two,
    )
    every_grad = reorder_all(every_grad, shard_count, group_count)
    shares = (
        lax.psum_scatter(every_grad[0], ("seq", "shard"), scatter_dimension=0, tiled=True),
        lax.psum_scatter(every_grad[1], ("seq", "shard"), scatter_dimension=0, tiled=True),
        lax.psum_scatter(every_grad[2], ("seq", "shard"), scatter_dimension=0, tiled=True),
        lax.psum_scatter(every_grad[3], ("seq", "shard"), scatter_dimension=0, tiled=True),
        lax.psum_scatter(every_grad[4], ("seq", "shard"), scatter_dimension=0, tiled=True),
        lax.psum_scatter(every_grad[5], ("seq", "shard"), scatter_dimension=0, tiled=True),
        lax.psum_scatter(every_grad[6], ("seq", "shard"), scatter_dimension=0, tiled=True),
        lax.psum_scatter(every_grad[7], ("seq", "shard"), scatter_dimension=0, tiled=True),
        lax.psum_scatter(every_grad[8], ("seq", "shard"), scatter_dimension=0, tiled=True),
        lax.psum_scatter(every_grad[9], ("seq", "shard"), scatter_dimension=0, tiled=True),
        lax.psum_scatter(every_grad[10], ("seq", "shard"), scatter_dimension=0, tiled=True),
        lax.psum_scatter(every_grad[11], ("seq", "shard"), scatter_dimension=0, tiled=True),
        lax.psum_scatter(every_grad[12], ("seq", "shard"), scatter_dimension=0, tiled=True),
    )
    (
        share_qkv,
        share_qbias,
        share_vbias,
        share_outw,
        share_outb,
        share_gain_one,
        share_shift_one,
        share_upw,
        share_upb,
        share_downw,
        share_downb,
        share_gain_two,
        share_shift_two,
    ) = shares
    summed = (
        lax.all_gather(share_qkv.astype(jnp.bfloat16), "seq", axis=0, tiled=True).astype(
            share_qkv.dtype
        ),
        lax.all_gather(share_qbias.astype(jnp.bfloat16), "seq", axis=0, tiled=True).astype(
            share_qbias.dtype
        ),
        lax.all_gather(share_vbias.astype(jnp.bfloat16), "seq", axis=0, tiled=True).astype(
            share_vbias.dtype
        ),
        lax.all_gather(share_outw.astype(jnp.bfloat16), "seq", axis=0, tiled=True).astype(
            share_outw.dtype
        ),
        lax.all_gather(share_outb.astype(jnp.bfloat16), "seq", axis=0, tiled=True).astype(
            share_outb.dtype
        ),
        lax.all_gather(share_gain_one.astype(jnp.bfloat16), "seq", axis=0, tiled=True).astype(
            share_gain_one.dtype
        ),
        lax.all_gather(share_shift_one.astype(jnp.bfloat16), "seq", axis=0, tiled=True).astype(
            share_shift_one.dtype
        ),
        lax.all_gather(share_upw.astype(jnp.bfloat16), "seq", axis=0, tiled=True).astype(
            share_upw.dtype
        ),
        lax.all_gather(share_upb.astype(jnp.bfloat16), "seq", axis=0, tiled=True).astype(
            share_upb.dtype
        ),
        lax.all_gather(share_downw.astype(jnp.bfloat16), "seq", axis=0, tiled=True).astype(
            share_downw.dtype
        ),
        lax.all_gather(share_downb.astype(jnp.bfloat16), "seq", axis=0, tiled=True).astype(
            share_downb.dtype
        ),
        lax.all_gather(share_gain_two.astype(jnp.bfloat16), "seq", axis=0, tiled=True).astype(
            share_gain_two.dtype
        ),
        lax.all_gather(share_shift_two.astype(jnp.bfloat16), "seq", axis=0, tiled=True).astype(
            share_shift_two.dtype
        ),
    )
    return (
        output,
        grad_input,
        summed[0],
        summed[1],
        summed[2],
        summed[3],
        summed[4],
        summed[5],
        summed[6],
        summed[7],
        summed[8],
        summed[9],
        summed[10],
        summed[11],
        summed[12],
    )


def solution(mesh):
    in_specs = (
        P("shard", "seq", None),
        P("shard"),
        P("shard", None),
        P("shard"),
        P("shard"),
        P("shard", None),
        P("shard"),
        P("shard"),
        P("shard"),
        P("shard", None),
        P("shard"),
        P("shard", None),
        P("shard"),
        P("shard"),
        P("shard"),
        P("shard", "seq", None),
    )
    out_specs = (
        P("shard", "seq", None),
        P("shard", "seq", None),
        P("shard", None),
        P("shard"),
        P("shard"),
        P("shard", None),
        P("shard"),
        P("shard"),
        P("shard"),
        P("shard", None),
        P("shard"),
        P("shard", None),
        P("shard"),
        P("shard"),
        P("shard"),
    )
    return jax.shard_map(
        per_device, mesh=mesh, in_specs=in_specs, out_specs=out_specs, check_vma=False
    )
```

profile of v0, /device:TPU:0, one launch (start us, length us, event | category | flops | bytes accessed | tf_op | source)
XLA Modules:
  0.0 979.9 jit_solution(11414818758463418126)
XLA Ops:
  18.0 32.2 %all-reduce.27 = (bf16[768]{0:T(1024)(128)(2,1)S(1)}, bf16[768]{0:T(1024)(128)(2,1)S(1)}, bf16[768]{0:T(1024)(128)(2,1)}, bf16[768]{0:T(1024)(128)(2,1)}, bf16[7...) all-reduce(bf16[768]{0:T(1024)(128)(2,1)S(1)} %dynamic-update-slice, ...), channel_id=1, replica_groups=mesh['seq'=4,'shard'=8] {'shard'}, use_global_device_ids=true, to_apply=%add.1 | all-reduce | flops 6144 | bytes 24576
  54.5 8.5 add_convert_fusion
  63.1 12.8 %reshape.544 = bf16[2,512,3,4,192]{4,3,2,1,0:T(4,128)(2,1)} reshape(bf16[1024,2304]{1,0:T(8,128)(2,1)} %add_convert_fusion) | data formatting | bytes 9437184 | tf_op jit(solution)/shard_map/reshape | solution.py:211
  75.9 17.4 %copy.144 = bf16[2,512,3,4,192]{1,0,4,2,3:T(2,128)(2,1)} copy(bf16[2,512,3,4,192]{4,3,2,1,0:T(4,128)(2,1)} %reshape.544) | data formatting | bytes 9437184 | tf_op jit(solution)/shard_map/reshape | solution.py:211
  99.6 52.5 %all-to-all-done = bf16[2,512,3,4,192]{1,0,4,2,3:T(2,128)(2,1)} async-done(((bf16[2,512,3,4,192]{1,0,4,2,3:T(2,128)(2,1)}), bf16[2,512,3,4,192]{1,0,4,2,3:T(2,128)(2,1)}, u32[]{:S(2)}, u32[]{:S(2)}) %all-to-all-start) | async-done | bytes 4718624 | tf_op jit(solution)/shard_map/all_to_all | solution.py:210
  152.1 10.6 %fusion.115 = (bf16[1,4,512,3,1,192]{2,0,5,3,1,4:T(2,128)(2,1)S(1)}, bf16[1,4,512,3,1,192]{2,0,5,3,1,4:T(2,128)(2,1)}) fusion(bf16[2,4,512,3,1,192]{2,0,5,3,1,4:T(2,128)(2,1)} %bitcast.3), kind=kLoop, calls=%fused_computation.175 | loop fusion | bytes 9437184 | tf_op jit(solution)/shard_map/slice | solution.py:221
  171.3 37.0 %while.56 = (s32[]{:T(128)}, bf16[4,512,3,64]{1,3,2,0:T(8,128)(2,1)S(1)}, f32[4,3,512]{2,1,0:T(4,128)S(1)}, bf16[4,512,3,64]{1,3,2,0:T(8,128)(2,1)S(1)}, bf16[20...) while((s32[]{:T(128)}, ...), condition=%wide.region_3.4_spmd.clone, body=%wide.region_0.3_spmd.clone.sunk | while | flops 843055616 | bytes 39979108 | solution.py:92
  208.3 7.7 copy.148
  216.0 5.9 squeeze.61
  227.4 39.2 %while.57 = (s32[]{:T(128)}, bf16[4,512,3,64]{1,3,2,0:T(8,128)(2,1)}, f32[4,3,512]{2,1,0:T(4,128)S(1)}, bf16[4,512,3,64]{1,3,2,0:T(8,128)(2,1)S(1)}, bf16[2048,3...) while((s32[]{:T(128)}, ...), condition=%wide.region_7.8_spmd.clone, body=%wide.region_4.7_spmd.clone.sunk | while | flops 843055616 | bytes 39975520 | solution.py:92
  276.9 6.1 copy.151
  287.7 12.7 %all-gather = bf16[8,1,384]{2,1,0:T(2,128)(2,1)S(1)} all-gather(bf16[1,1,384]{2,1,0:T(2,128)(2,1)S(1)} %reshape.506), channel_id=1, replica_groups=mesh['seq'=4,'shard'=8] {'shard'}, dimensions={0}, use_global_device_ids=true | all-gather | bytes 6912 | tf_op jit(solution)/shard_map/all_gather | solution.py:180
  301.8 10.6 %all-to-all-done.1 = bf16[2,2048,1,192]{3,0,2,1:T(2,128)(2,1)} async-done(((bf16[2,2048,1,192]{3,0,2,1:T(2,128)(2,1)}), bf16[2,2048,1,192]{3,0,2,1:T(2,128)(2,1)}, u32[]{:S(2)}, u32[]{:S(2)}) %all-to-all-start.1) | async-done | bytes 1572896 | tf_op jit(solution)/shard_map/all_to_all | solution.py:227
  312.4 6.1 copy.178
  326.1 12.1 %multiply_convert_fusion.2 = (bf16[1024,3072]{1,0:T(8,128)(2,1)}, f32[1024,3072]{1,0:T(8,128)}) fusion(f32[3072]{0:T(1024)S(1)} %bitcast.340, bf16[768,3072]{1,0:T(8,128)(2,1)} %all-gather.10.cloned.1.call-done, f32[1024,768]{1,0:T(8,128)S(1)} %get-tuple-element.615, f32[768]{0:T(1024)S(1)} %convert_element_type.210, f32[768]{0:T(1024)S(1)} %convert_element_type.209, ...), kind=kOutput, calls=%fused_computation.108 | convolution fusion | flops 4854644736 | bytes 26765312 | tf_op jit(solution)/shard_map/dot_general | solution.py:237
  338.2 8.8 fusion.119
  353.1 13.9 %convert_reduce_fusion = (f32[3072]{0:T(1024)}, bf16[1024,3072]{1,0:T(8,128)(2,1)S(1)}) fusion(f32[1024,3072]{1,0:T(8,128)} %get-tuple-element.617, f32[3072]{0:T(1024)S(1)} %bitcast.341, bf16[3072,768]{1,0:T(8,128)(2,1)S(1)} %copy-done.47, f32[1024,768]{1,0:T(8,128)S(1)} %get-tuple-element.590), kind=kOutput, calls=%fused_computation.107 | convolution fusion | flops 4873516032 | bytes 26763264 | tf_op jit(solution)/shard_map/dot_general | solution.py:20
  367.0 6.5 multiply_reduce_fusion.2
  378.7 7.9 fusion.110
  404.3 8.9 fusion.107
  428.1 130.5 %while.58 = (s32[]{:T(128)}, f32[2048,3,64]{0,2,1:T(8,128)}, f32[2048,3,64]{0,2,1:T(8,128)}, bf16[4,512,3,64]{1,3,2,0:T(8,128)(2,1)}, bf16[4,512,3,64]{1,3,2,0:T...) while((s32[]{:T(128)}, f32[2048,3,64]{0,2,1:T(8,128)}, ...), condition=%wide.region_18.19_spmd.clone, body=%wide.region_16.18_spmd.clone.sunk | while | flops 2062516736 | bytes 204919504 | solution.py:136
  432.4 5.8 multiply_reduce_fusion.9
  448.7 6.2 fusion.211
  474.8 5.8 fusion.209
  480.6 6.2 fusion.211
  496.5 5.8 multiply_reduce_fusion.9
  507.4 6.2 fusion.209
  513.6 6.7 fusion.211
  540.8 5.9 fusion.209
  546.7 6.4 fusion.211
  562.0 122.0 %while.59 = (s32[]{:T(128)}, f32[2048,3,64]{0,2,1:T(8,128)S(1)}, f32[2048,3,64]{0,2,1:T(8,128)}, bf16[4,512,3,64]{1,3,2,0:T(8,128)(2,1)}, bf16[4,512,3,64]{1,3,2...) while((s32[]{:T(128)}, f32[2048,3,64]{0,2,1:T(8,128)S(1)}, ...), condition=%wide.region_21.22_spmd.clone, body=%wide.region_19.21_spmd.clone.sunk | while | flops 2062516736 | bytes 214356272 | solution.py:136
  616.5 5.8 fusion.223
  641.3 6.0 fusion.224
  647.3 5.9 fusion.223
  671.8 6.4 fusion.224
  678.2 5.8 fusion.223
  701.5 16.1 %copy.159 = bf16[2,2048,3,1,192]{4,0,3,2,1:T(2,128)(2,1)} copy(bf16[2,2048,3,1,192]{1,4,3,2,0:T(8,128)(2,1)} %maximum_maximum_fusion) | data formatting | bytes 9437184 | tf_op jit(solution)/shard_map/stack | solution.py:282
  717.6 81.4 %all_to_all.60 = bf16[2,2048,3,1,192]{4,0,3,2,1:T(2,128)(2,1)} all-to-all(bf16[2,2048,3,1,192]{4,0,3,2,1:T(2,128)(2,1)} %copy.159), channel_id=1, replica_groups=mesh['seq'=4,'shard'=8] {'seq'}, dimensions={1} | all-to-all | bytes 9437184 | tf_op jit(solution)/shard_map/all_to_all | solution.py:283
  799.0 16.9 %copy.179 = bf16[2,4,512,3,1,192]{2,1,5,3,0,4:T(4,128)(2,1)} copy(bf16[2,4,512,3,1,192]{5,0,3,2,1,4:T(2,128)(2,1)} %bitcast.309) | data formatting | bytes 9437184 | tf_op jit(solution)/shard_map/all_to_all | solution.py:283
  815.9 9.4 copy.161
  841.8 9.0 all_gather.94
  854.4 40.1 %all-reduce.26 = (bf16[768]{0:T(1024)(128)(2,1)S(1)}, bf16[768]{0:T(1024)(128)(2,1)S(1)}, bf16[768]{0:T(1024)(128)(2,1)S(1)}, bf16[768]{0:T(1024)(128)(2,1)S(1)}...) all-reduce(f32[768]{0:T(1024)S(1)} %reshape.432, ...), channel_id=3, replica_groups=mesh['seq'=4,'shard'=8] {'seq','shard'}, use_global_device_ids=true, to_apply=%region_24.25.clone | all-reduce | flops 9216 | bytes 55296
  897.2 9.9 %all-reduce.28 = (bf16[96]{0:T(256)(128)(2,1)S(1)}, bf16[96]{0:T(256)(128)(2,1)S(1)}, bf16[96]{0:T(256)(128)(2,1)S(1)}, bf16[96]{0:T(256)(128)(2,1)S(1)}, bf16[9...) all-reduce(bf16[96]{0:T(256)(128)(2,1)S(1)} %dynamic-update-slice.8, ...), channel_id=1, replica_groups=mesh['seq'=4,'shard'=8] {'seq'}, use_global_device_ids=true, to_apply=%add.8 | all-reduce | flops 1152 | bytes 4608
  911.8 8.5 add_convert_fusion.1
  921.3 12.6 %all_gather.98 = bf16[96,3072]{1,0:T(8,128)(2,1)S(1)} all-gather(bf16[24,3072]{1,0:T(8,128)(2,1)S(1)} %convert_element_type.243), channel_id=1, replica_groups=mesh['seq'=4,'shard'=8] {'seq'}, dimensions={0}, use_global_device_ids=true | all-gather | bytes 737280 | tf_op jit(solution)/shard_map/all_gather | solution.py:364
  936.0 10.4 %all_gather.100 = bf16[384,768]{1,0:T(8,128)(2,1)S(1)} all-gather(bf16[96,768]{1,0:T(8,128)(2,1)S(1)} %convert_element_type.248), channel_id=1, replica_groups=mesh['seq'=4,'shard'=8] {'seq'}, dimensions={0}, use_global_device_ids=true | all-gather | bytes 737280 | tf_op jit(solution)/shard_map/all_gather | solution.py:370
  947.5 12.9 %reduce-scatter.5.cloned.1.call-done = f32[24,2304]{1,0:T(8,128)} async-done(((f32[768,2304]{1,0:T(8,128)}), f32[24,2304]{1,0:T(8,128)}) %reduce-scatter.5.cloned.1.call-update) | async-done | bytes 221200 | tf_op jit(solution)/shard_map/reduce_scatter | solution.py:313
  961.3 10.3 %all_gather.91 = bf16[96,2304]{1,0:T(8,128)(2,1)S(1)} all-gather(bf16[24,2304]{1,0:T(8,128)(2,1)S(1)} %convert_element_type.226), channel_id=1, replica_groups=mesh['seq'=4,'shard'=8] {'seq'}, dimensions={0}, use_global_device_ids=true | all-gather | bytes 552960 | tf_op jit(solution)/shard_map/all_gather | solution.py:343
  (427 shorter events, 397.8 us)
Async XLA Ops:
  7.2 47.3 %all-gather.6.cloned.1.call-start = ((), (), s32[]{:S(2)}) async-start(), calls=%async_computation.8 | async-start | bytes 3981312 | tf_op jit(solution)/shard_map/all_gather | solution.py:172
  7.9 313.8 %all-gather.8.cloned.1.call-start = ((), (), s32[]{:S(2)}) async-start(), calls=%async_computation.9 | async-start | bytes 1327104 | tf_op jit(solution)/shard_map/all_gather | solution.py:175
  8.7 317.4 %all-gather.10.cloned.1.call-start = ((), (), s32[]{:S(2)}) async-start(), calls=%async_computation.10 | async-start | bytes 5308416 | tf_op jit(solution)/shard_map/all_gather | solution.py:179
  93.3 58.8 %all-to-all-start = ((bf16[2,512,3,4,192]{1,0,4,2,3:T(2,128)(2,1)}), bf16[2,512,3,4,192]{1,0,4,2,3:T(2,128)(2,1)}, u32[]{:S(2)}, u32[]{:S(2)}) async-start(bf16[2,512,3,4,192]{1,0,4,2,3:T(2,128)(2,1)} %copy.144), calls=%async_computation | async-start | bytes 9437184 | tf_op jit(solution)/shard_map/all_to_all | solution.py:210
  98.4 239.8 %all-gather.12.cloned.1.call-start = ((), (), s32[]{:S(2)}) async-start(), calls=%async_computation.11 | async-start | bytes 5308416 | tf_op jit(solution)/shard_map/all_gather | solution.py:181
  208.3 7.7 copy-start.6
  208.3 7.7 copy-start.12
  208.3 7.7 copy-start.14
  208.3 7.7 copy-start.30
  266.5 10.3 %copy-start.4 = (bf16[2048,3,64]{0,2,1:T(8,128)(2,1)}, bf16[2048,3,64]{0,2,1:T(8,128)(2,1)S(1)}, u32[]{:S(2)}) copy-start(bf16[2048,3,64]{0,2,1:T(8,128)(2,1)S(1)} %get-tuple-element.977) | copy-start | bytes 2359300
  266.5 10.3 %copy-start.10 = (bf16[2048,3,64]{0,2,1:T(8,128)(2,1)}, bf16[2048,3,64]{0,2,1:T(8,128)(2,1)S(1)}, u32[]{:S(2)}) copy-start(bf16[2048,3,64]{0,2,1:T(8,128)(2,1)S(1)} %get-tuple-element.979) | copy-start | bytes 2359300
  266.5 10.3 %copy-start.13 = (bf16[4,512,3,64]{1,3,2,0:T(8,128)(2,1)}, bf16[4,512,3,64]{1,3,2,0:T(8,128)(2,1)S(1)}, u32[]{:S(2)}) copy-start(bf16[4,512,3,64]{1,3,2,0:T(8,128)(2,1)S(1)} %get-tuple-element.989) | copy-start | bytes 2359300
  266.5 10.3 %copy-start.31 = (f32[4,3,512]{2,1,0:T(4,128)}, f32[4,3,512]{2,1,0:T(4,128)S(1)}, u32[]{:S(2)}) copy-start(f32[4,3,512]{2,1,0:T(4,128)S(1)} %get-tuple-element.903) | copy-start | bytes 73732
  276.9 10.8 %copy-start.44 = (bf16[768]{0:T(1024)(128)(2,1)S(1)}, bf16[768]{0:T(1024)(128)(2,1)}, u32[]{:S(2)}) copy-start(bf16[768]{0:T(1024)(128)(2,1)} %get-tuple-element.574) | copy-start | bytes 4612
  276.9 10.8 %copy-start.43 = (bf16[768]{0:T(1024)(128)(2,1)S(1)}, bf16[768]{0:T(1024)(128)(2,1)}, u32[]{:S(2)}) copy-start(bf16[768]{0:T(1024)(128)(2,1)} %get-tuple-element.576) | copy-start | bytes 4612
  276.9 10.8 %copy-start.42 = (bf16[768]{0:T(1024)(128)(2,1)S(1)}, bf16[768]{0:T(1024)(128)(2,1)}, u32[]{:S(2)}) copy-start(bf16[768]{0:T(1024)(128)(2,1)} %get-tuple-element.575) | copy-start | bytes 4612
  276.9 10.8 %copy-start.46 = (bf16[384]{0:T(512)(128)(2,1)S(1)}, bf16[384]{0:T(512)(128)(2,1)}, u32[]{:S(2)}) copy-start(bf16[384]{0:T(512)(128)(2,1)} %param.34) | copy-start | bytes 2308
  276.9 23.5 %copy-start.41 = (bf16[768]{0:T(1024)(128)(2,1)S(1)}, bf16[768]{0:T(1024)(128)(2,1)}, u32[]{:S(2)}) copy-start(bf16[768]{0:T(1024)(128)(2,1)} %get-tuple-element.577) | copy-start | bytes 4612
  276.9 23.5 %copy-start.40 = (bf16[768]{0:T(1024)(128)(2,1)S(1)}, bf16[768]{0:T(1024)(128)(2,1)}, u32[]{:S(2)}) copy-start(bf16[768]{0:T(1024)(128)(2,1)} %get-tuple-element.579) | copy-start | bytes 4612
  283.0 17.5 %copy-start.15 = (bf16[2,512,768]{2,1,0:T(8,128)(2,1)S(1)}, bf16[2,512,768]{2,1,0:T(8,128)(2,1)}, u32[]{:S(2)}) copy-start(bf16[2,512,768]{2,1,0:T(8,128)(2,1)} %param.39) | copy-start | bytes 4718596
  283.0 18.8 %copy-start.39 = (bf16[768]{0:T(1024)(128)(2,1)S(1)}, bf16[768]{0:T(1024)(128)(2,1)}, u32[]{:S(2)}) copy-start(bf16[768]{0:T(1024)(128)(2,1)} %get-tuple-element.578) | copy-start | bytes 4612
  283.0 29.3 %all-to-all-start.1 = ((bf16[2,2048,1,192]{3,0,2,1:T(2,128)(2,1)}), bf16[2,2048,1,192]{3,0,2,1:T(2,128)(2,1)}, u32[]{:S(2)}, u32[]{:S(2)}) async-start(bf16[2,2048,1,192]{3,0,2,1:T(2,128)(2,1)} %copy.151), calls=%async_computation.1 | async-start | bytes 4194304 | tf_op jit(solution)/shard_map/all_to_all | solution.py:227
  287.6 553.3 %reduce-scatter.7.cloned.1.call-start = ((), (), s32[]{:S(2)}) async-start(), calls=%async_computation.13 | async-start | bytes 2433024 | tf_op jit(solution)/shard_map/reduce_scatter | solution.py:316
  350.2 16.8 %slice-start = ((s8[4718592]{0:T(1024)(128)(4,1)}), s8[4194304]{0:T(1024)(128)(4,1)S(1)}, s32[]{:S(2)}) async-start(s8[4718592]{0:T(1024)(128)(4,1)} %bitcast.342), calls=%async_computation.16 | async-start | bytes 8388608
  353.1 13.9 %copy-start.19 = (f32[1024,768]{1,0:T(8,128)}, f32[1024,768]{1,0:T(8,128)S(1)}, u32[]{:S(2)}) copy-start(f32[1024,768]{1,0:T(8,128)S(1)} %get-tuple-element.590) | copy-start | bytes 9437188
  353.1 13.9 %slice-start.1 = ((s8[4718592]{0:T(1024)(128)(4,1)}), s8[524288]{0:T(1024)(128)(4,1)S(1)}, s32[]{:S(2)}) async-start(s8[4718592]{0:T(1024)(128)(4,1)} %bitcast.342), calls=%async_computation.17 | async-start | bytes 1048576
  378.7 541.6 %reduce-scatter.9.cloned.1.call-start = ((), (), s32[]{:S(2)}) async-start(), calls=%async_computation.14 | async-start | bytes 9732096 | tf_op jit(solution)/shard_map/reduce_scatter | solution.py:320
  400.7 22.2 %all-to-all-start.2 = ((bf16[2,512,4,192]{1,0,3,2:T(2,128)(2,1)}), bf16[2,512,4,192]{1,0,3,2:T(2,128)(2,1)S(1)}, u32[]{:S(2)}, u32[]{:S(2)}) async-start(bf16[2,512,4,192]{1,0,3,2:T(2,128)(2,1)} %reshape.426), calls=%async_computation.2 | async-start | bytes 3145728 | tf_op jit(solution)/shard_map/all_to_all | solution.py:263
  404.3 530.7 %reduce-scatter.11.cloned.1.call-start = ((), (), s32[]{:S(2)}) async-start(), calls=%async_computation.15 | async-start | bytes 9732096 | tf_op jit(solution)/shard_map/reduce_scatter | solution.py:322
  417.9 542.4 %reduce-scatter.5.cloned.1.call-start = ((), (), s32[]{:S(2)}) async-start(), calls=%async_computation.12 | async-start | bytes 7299072 | tf_op jit(solution)/shard_map/reduce_scatter | solution.py:313
  428.1 134.0 %copy-start.5 = (bf16[2048,3,64]{0,2,1:T(8,128)(2,1)S(1)}, bf16[2048,3,64]{0,2,1:T(8,128)(2,1)}, u32[]{:S(2)}) copy-start(bf16[2048,3,64]{0,2,1:T(8,128)(2,1)} %copy-done.4) | copy-start | bytes 2359300
  428.1 134.0 %copy-start.8 = (f32[2048,3,64]{0,2,1:T(8,128)S(1)}, f32[2048,3,64]{0,2,1:T(8,128)}, u32[]{:S(2)}) copy-start(f32[2048,3,64]{0,2,1:T(8,128)} %custom-call.2) | copy-start | bytes 4718596
  431.0 7.3 copy-start
  443.2 11.7 %copy-start.1 = (f32[3,512,2048]{2,1,0:T(8,128)S(1)}, f32[3,512,2048]{2,1,0:T(8,128)}, u32[]{:S(2)}) copy-start(f32[3,512,2048]{2,1,0:T(8,128)} %copy-done) | copy-start | bytes 37748740 | tf_op jit(solution)/shard_map/while
  474.8 12.0 %copy-start.1 = (f32[3,512,2048]{2,1,0:T(8,128)S(1)}, f32[3,512,2048]{2,1,0:T(8,128)}, u32[]{:S(2)}) copy-start(f32[3,512,2048]{2,1,0:T(8,128)} %copy-done) | copy-start | bytes 37748740 | tf_op jit(solution)/shard_map/while
  495.1 7.3 copy-start
  507.4 12.9 %copy-start.1 = (f32[3,512,2048]{2,1,0:T(8,128)S(1)}, f32[3,512,2048]{2,1,0:T(8,128)}, u32[]{:S(2)}) copy-start(f32[3,512,2048]{2,1,0:T(8,128)} %copy-done) | copy-start | bytes 37748740 | tf_op jit(solution)/shard_map/while
  528.6 7.2 copy-start
  540.8 12.2 %copy-start.1 = (f32[3,512,2048]{2,1,0:T(8,128)S(1)}, f32[3,512,2048]{2,1,0:T(8,128)}, u32[]{:S(2)}) copy-start(f32[3,512,2048]{2,1,0:T(8,128)} %copy-done) | copy-start | bytes 37748740 | tf_op jit(solution)/shard_map/while
  571.4 9.9 %copy-start.23 = (bf16[4,512,3,64]{1,3,2,0:T(8,128)(2,1)S(1)}, bf16[4,512,3,64]{1,3,2,0:T(8,128)(2,1)}, u32[]{:S(2)}) copy-start(bf16[4,512,3,64]{1,3,2,0:T(8,128)(2,1)} %get-tuple-element.912) | copy-start | bytes 2359300 | tf_op jit(solution)/shard_map/while
  576.4 10.5 %copy-start.3 = (f32[3,512,2048]{2,1,0:T(8,128)S(1)}, f32[3,512,2048]{2,1,0:T(8,128)}, u32[]{:S(2)}) copy-start(f32[3,512,2048]{2,1,0:T(8,128)} %copy-done.2) | copy-start | bytes 37748740 | tf_op jit(solution)/shard_map/while
  601.4 9.4 copy-start.23
  606.4 10.1 %copy-start.3 = (f32[3,512,2048]{2,1,0:T(8,128)S(1)}, f32[3,512,2048]{2,1,0:T(8,128)}, u32[]{:S(2)}) copy-start(f32[3,512,2048]{2,1,0:T(8,128)} %copy-done.2) | copy-start | bytes 37748740 | tf_op jit(solution)/shard_map/while
  631.6 9.7 copy-start.23
  636.6 10.7 %copy-start.3 = (f32[3,512,2048]{2,1,0:T(8,128)S(1)}, f32[3,512,2048]{2,1,0:T(8,128)}, u32[]{:S(2)}) copy-start(f32[3,512,2048]{2,1,0:T(8,128)} %copy-done.2) | copy-start | bytes 37748740 | tf_op jit(solution)/shard_map/while
  662.4 9.4 copy-start.23
  667.4 10.8 %copy-start.3 = (f32[3,512,2048]{2,1,0:T(8,128)S(1)}, f32[3,512,2048]{2,1,0:T(8,128)}, u32[]{:S(2)}) copy-start(f32[3,512,2048]{2,1,0:T(8,128)} %copy-done.2) | copy-start | bytes 37748740 | tf_op jit(solution)/shard_map/while
  837.0 74.7 %copy-start.28 = (f32[1024,768]{1,0:T(8,128)S(1)}, f32[1024,768]{1,0:T(8,128)}, u32[]{:S(2)}) copy-start(f32[1024,768]{1,0:T(8,128)} %copy-done.26) | copy-start | bytes 9437188
  (36 other events, 145.8 us)
Sparse Core Ops, SparseCore 0:
  9.7 44.8 all-gather.5
  56.2 21.5 all-gather.7
  79.4 51.4 all-gather.9
  132.4 50.5 all-gather.11
  378.8 97.0 reduce-scatter.6
  482.7 134.6 reduce-scatter.8
  623.2 153.8 reduce-scatter.10
  837.2 123.1 reduce-scatter.4
where the time goes:
time: 990 us; the launch traced here: 980 us
  matrix products  337 us (34%)
  blocking collectives  219 us (22%)
  local copies, waits for them, and re-layouts  197 us (20%)
  other arithmetic  107 us (11%)
  waiting for transfers between devices  87.7 us (9%)
  between operations  17.5 us (2%)
  starting transfers between devices  13.8 us (1%)
    unnamed x3, blocking collectives  82.3 us
    all_to_all x1, blocking collectives, per_device(): lax.all_to_all(grad_qkv_heads, 'seq', split_axis=1, concat_axis=3, tiled=...  81.4 us
    all_to_all x1, waiting for transfers between devices, per_device(): lax.all_to_all(qkv_tok.reshape(seq_count, pos_count, 3, group_count, grou...  52.5 us
    dot_general x8, matrix products, one_block(): jnp.einsum('hbk,khd->bhd', grad_scores, keys_all, preferred_element_type=...  48.9 us
    dot_general x8, matrix products, one_block(): jnp.einsum('hbk,bhd->khd', attn_prob.astype(jnp.bfloat16), grad_blk, pref...  44.2 us
    dot_general x8, matrix products, one_block(): jnp.einsum('bhd,khd->hbk', grad_blk, values_all, preferred_element_type=j...  42.9 us
    dot_general x8, matrix products, one_block(): jnp.einsum('hbk,bhd->khd', grad_scores, query_blk, preferred_element_type...  41.9 us
    convert_element_type x8, other arithmetic, one_block(): grad_scores = (attn_prob * (grad_prob - row_dot)).astype(jnp.bfloat16)  39.8 us
  transfers between devices with their start and end apart: 11, of which 5 were waited for; matrix products, arithmetic and copies ran while one was open for 61% of the time, Pallas kernels for 0%

commit v1 on v0

--- a/solution.py
+++ b/solution.py
@@ -224,8 +224,11 @@
     attended_heads = (
         jnp.stack(attended_list).astype(jnp.bfloat16).reshape(seq_count, full_len, 1, group_width)
     )
-    attended = lax.all_to_all(
-        attended_heads, "seq", split_axis=1, concat_axis=2, tiled=True
+    attended = jnp.concatenate(
+        lax.all_to_all(
+            jnp.stack(jnp.split(attended_heads, lax.axis_size("seq"), axis=1)), "seq", 0, 0
+        ),
+        axis=2,
     ).reshape(tok_count, model_width)
     projected = jnp.dot(attended, out_weight, preferred_element_type=jnp.float32) + out_bias.astype(
         jnp.float32

time: 990 us -> 971 us (0.981)
  matrix products: 337 us -> 326 us
    unnamed x144 -> x133, local copies, waits for them, and re-layouts: 25.6 us -> 25.7 us
  transfers between devices with their start and end apart: 11 -> 11, of which waited for: 5 -> 5; matrix products, arithmetic and copies ran while one was open for 61% -> 60% of each run, Pallas kernels for 0% -> 0%
where the time goes in v1:
time: 971 us; the launch traced here: 961 us
  matrix products  326 us (34%)
  blocking collectives  224 us (23%)
  local copies, waits for them, and re-layouts  190 us (20%)
  other arithmetic  109 us (11%)
  waiting for transfers between devices  80.1 us (8%)
  between operations  17.5 us (2%)
  starting transfers between devices  14.5 us (1%)
    all_to_all x1, blocking collectives, per_device(): lax.all_to_all(grad_qkv_heads, 'seq', split_axis=1, concat_axis=3, tiled=...  87 us
    unnamed x3, blocking collectives  82.3 us
    all_to_all x1, waiting for transfers between devices, per_device(): lax.all_to_all(qkv_tok.reshape(seq_count, pos_count, 3, group_count, grou...  52.5 us
    dot_general x8, matrix products, one_block(): jnp.einsum('hbk,khd->bhd', grad_scores, keys_all, preferred_element_type=...  51.3 us
    dot_general x8, matrix products, one_block(): jnp.einsum('hbk,bhd->khd', attn_prob.astype(jnp.bfloat16), grad_blk, pref...  41.2 us
    dot_general x8, matrix products, one_block(): jnp.einsum('hbk,bhd->khd', grad_scores, query_blk, preferred_element_type...  41 us
    convert_element_type x8, other arithmetic, one_block(): grad_scores = (attn_prob * (grad_prob - row_dot)).astype(jnp.bfloat16)  39.6 us
    dot_general x8, matrix products, one_block(): jnp.einsum('bhd,khd->hbk', grad_blk, values_all, preferred_element_type=j...  34.7 us
  transfers between devices with their start and end apart: 11, of which 5 were waited for; matrix products, arithmetic and copies ran while one was open for 60% of the time, Pallas kernels for 0%

profile of v1, /device:TPU:0, one launch (start us, length us, event | category | flops | bytes accessed | tf_op | source)
XLA Modules:
  0.0 961.1 jit_solution(6716818135580783000)
XLA Ops:
  18.0 32.2 %all-reduce.27 = (bf16[768]{0:T(1024)(128)(2,1)S(1)}, bf16[768]{0:T(1024)(128)(2,1)S(1)}, bf16[768]{0:T(1024)(128)(2,1)}, bf16[768]{0:T(1024)(128)(2,1)}, bf16[7...) all-reduce(bf16[768]{0:T(1024)(128)(2,1)S(1)} %dynamic-update-slice, ...), channel_id=1, replica_groups=mesh['seq'=4,'shard'=8] {'shard'}, use_global_device_ids=true, to_apply=%add.1 | all-reduce | flops 6144 | bytes 24576
  54.5 8.5 add_convert_fusion
  63.0 12.8 %reshape.543 = bf16[2,512,3,4,192]{4,3,2,1,0:T(4,128)(2,1)} reshape(bf16[1024,2304]{1,0:T(8,128)(2,1)} %add_convert_fusion) | data formatting | bytes 9437184 | tf_op jit(solution)/shard_map/reshape | solution.py:211
  75.9 17.4 %copy.155 = bf16[2,512,3,4,192]{1,0,4,2,3:T(2,128)(2,1)} copy(bf16[2,512,3,4,192]{4,3,2,1,0:T(4,128)(2,1)} %reshape.543) | data formatting | bytes 9437184 | tf_op jit(solution)/shard_map/reshape | solution.py:211
  99.6 52.5 %all-to-all-done = bf16[2,512,3,4,192]{1,0,4,2,3:T(2,128)(2,1)} async-done(((bf16[2,512,3,4,192]{1,0,4,2,3:T(2,128)(2,1)}), bf16[2,512,3,4,192]{1,0,4,2,3:T(2,128)(2,1)}, u32[]{:S(2)}, u32[]{:S(2)}) %all-to-all-start) | async-done | bytes 4718624 | tf_op jit(solution)/shard_map/all_to_all | solution.py:210
  152.0 10.6 %fusion.115 = (bf16[1,4,512,3,1,192]{2,0,5,3,1,4:T(2,128)(2,1)S(1)}, bf16[1,4,512,3,1,192]{2,0,5,3,1,4:T(2,128)(2,1)}) fusion(bf16[2,4,512,3,1,192]{2,0,5,3,1,4:T(2,128)(2,1)} %bitcast.3), kind=kLoop, calls=%fused_computation.181 | loop fusion | bytes 9437184 | tf_op jit(solution)/shard_map/slice | solution.py:221
  171.2 37.0 %while.57 = (s32[]{:T(128)}, bf16[4,512,3,64]{1,3,2,0:T(8,128)(2,1)S(1)}, f32[4,3,512]{2,1,0:T(4,128)S(1)}, bf16[4,512,3,64]{1,3,2,0:T(8,128)(2,1)S(1)}, bf16[20...) while((s32[]{:T(128)}, ...), condition=%wide.region_7.8_spmd.clone, body=%wide.region_4.7_spmd.clone.sunk | while | flops 843055616 | bytes 39979108 | solution.py:92
  208.3 7.6 copy.156
  216.0 5.9 squeeze.57
  227.3 39.2 %while.56 = (s32[]{:T(128)}, bf16[4,512,3,64]{1,3,2,0:T(8,128)(2,1)}, f32[4,3,512]{2,1,0:T(4,128)S(1)}, bf16[4,512,3,64]{1,3,2,0:T(8,128)(2,1)S(1)}, bf16[2048,3...) while((s32[]{:T(128)}, ...), condition=%wide.region_3.4_spmd.clone, body=%wide.region_0.3_spmd.clone.sunk | while | flops 843055616 | bytes 39975520 | solution.py:92
  283.4 12.7 %all-gather = bf16[8,1,384]{2,1,0:T(2,128)(2,1)S(1)} all-gather(bf16[1,1,384]{2,1,0:T(2,128)(2,1)S(1)} %reshape.505), channel_id=1, replica_groups=mesh['seq'=4,'shard'=8] {'shard'}, dimensions={0}, use_global_device_ids=true | all-gather | bytes 6912 | tf_op jit(solution)/shard_map/all_gather | solution.py:180
  313.1 12.6 %multiply_convert_fusion.2 = (bf16[1024,3072]{1,0:T(8,128)(2,1)}, f32[1024,3072]{1,0:T(8,128)}) fusion(f32[3072]{0:T(1024)S(1)} %bitcast.349, bf16[768,3072]{1,0:T(8,128)(2,1)} %all-gather.10.cloned.1.call-done, f32[1024,768]{1,0:T(8,128)} %copy-done.9, f32[768]{0:T(1024)S(1)} %convert_element_type.210, f32[768]{0:T(1024)S(1)} %convert_element_type.209, ...), kind=kOutput, calls=%fused_computation.108 | convolution fusion | flops 4854644736 | bytes 26765312 | tf_op jit(solution)/shard_map/dot_general | solution.py:240
  325.6 9.3 fusion.119
  341.0 13.7 %convert_reduce_fusion = (f32[3072]{0:T(1024)}, bf16[1024,3072]{1,0:T(8,128)(2,1)S(1)}) fusion(f32[1024,3072]{1,0:T(8,128)} %get-tuple-element.620, f32[3072]{0:T(1024)S(1)} %bitcast.350, bf16[3072,768]{1,0:T(8,128)(2,1)S(1)} %copy-done.38, f32[1024,768]{1,0:T(8,128)S(1)} %get-tuple-element.590), kind=kOutput, calls=%fused_computation.107 | convolution fusion | flops 4873516032 | bytes 26763264 | tf_op jit(solution)/shard_map/dot_general | solution.py:20
  354.8 6.5 multiply_reduce_fusion.2
  366.4 8.9 fusion.110
  395.4 8.5 fusion.107
  408.6 5.5 all-to-all-done.2
  414.1 5.6 fusion.116
  420.9 113.5 %while.58 = (s32[]{:T(128)}, f32[2048,3,64]{0,2,1:T(8,128)}, f32[2048,3,64]{0,2,1:T(8,128)}, bf16[4,512,3,64]{1,3,2,0:T(8,128)(2,1)}, bf16[4,512,3,64]{1,3,2,0:T...) while((s32[]{:T(128)}, f32[2048,3,64]{0,2,1:T(8,128)}, ...), condition=%wide.region_18.19_spmd.clone, body=%wide.region_16.18_spmd.clone.sunk | while | flops 2062516736 | bytes 204921552 | solution.py:136
  432.2 5.3 fusion.209
  437.5 6.2 fusion.211
  459.0 5.8 fusion.209
  464.8 6.2 fusion.211
  487.8 6.1 fusion.209
  493.9 6.6 fusion.211
  517.2 5.7 fusion.209
  522.9 6.2 fusion.211
  538.0 122.5 %while.59 = (s32[]{:T(128)}, f32[2048,3,64]{0,2,1:T(8,128)S(1)}, f32[2048,3,64]{0,2,1:T(8,128)}, bf16[4,512,3,64]{1,3,2,0:T(8,128)(2,1)}, bf16[4,512,3,64]{1,3,2...) while((s32[]{:T(128)}, f32[2048,3,64]{0,2,1:T(8,128)S(1)}, ...), condition=%wide.region_21.22_spmd.clone, body=%wide.region_19.21_spmd.clone.sunk | while | flops 2062516736 | bytes 204919504 | solution.py:136
  556.7 6.5 fusion.224
  586.7 6.2 fusion.224
  593.0 5.5 fusion.223
  617.2 6.7 fusion.224
  623.9 5.6 fusion.223
  648.4 6.6 fusion.224
  655.0 5.5 fusion.223
  678.3 16.1 %copy.171 = bf16[2,2048,3,1,192]{4,0,3,2,1:T(2,128)(2,1)} copy(bf16[2,2048,3,1,192]{1,4,3,2,0:T(8,128)(2,1)} %maximum_maximum_fusion) | data formatting | bytes 9437184 | tf_op jit(solution)/shard_map/stack | solution.py:285
  694.4 87.0 %all_to_all.50 = bf16[2,2048,3,1,192]{4,0,3,2,1:T(2,128)(2,1)} all-to-all(bf16[2,2048,3,1,192]{4,0,3,2,1:T(2,128)(2,1)} %copy.171), channel_id=1, replica_groups=mesh['seq'=4,'shard'=8] {'seq'}, dimensions={1} | all-to-all | bytes 9437184 | tf_op jit(solution)/shard_map/all_to_all | solution.py:286
  781.4 16.9 %copy.190 = bf16[2,4,512,3,1,192]{2,1,5,3,0,4:T(4,128)(2,1)} copy(bf16[2,4,512,3,1,192]{5,0,3,2,1,4:T(2,128)(2,1)} %bitcast.319) | data formatting | bytes 9437184 | tf_op jit(solution)/shard_map/all_to_all | solution.py:286
  798.4 9.4 copy.173
  824.3 8.8 all_gather.94
  836.6 40.2 %all-reduce.26 = (bf16[768]{0:T(1024)(128)(2,1)S(1)}, bf16[768]{0:T(1024)(128)(2,1)S(1)}, bf16[768]{0:T(1024)(128)(2,1)S(1)}, bf16[768]{0:T(1024)(128)(2,1)S(1)}...) all-reduce(f32[768]{0:T(1024)S(1)} %reshape.431, ...), channel_id=3, replica_groups=mesh['seq'=4,'shard'=8] {'seq','shard'}, use_global_device_ids=true, to_apply=%region_24.25.clone | all-reduce | flops 9216 | bytes 55296
  879.5 9.9 %all-reduce.28 = (bf16[96]{0:T(256)(128)(2,1)S(1)}, bf16[96]{0:T(256)(128)(2,1)S(1)}, bf16[96]{0:T(256)(128)(2,1)S(1)}, bf16[96]{0:T(256)(128)(2,1)S(1)}, bf16[9...) all-reduce(bf16[96]{0:T(256)(128)(2,1)S(1)} %dynamic-update-slice.8, ...), channel_id=1, replica_groups=mesh['seq'=4,'shard'=8] {'seq'}, use_global_device_ids=true, to_apply=%add.8 | all-reduce | flops 1152 | bytes 4608
  894.0 8.5 add_convert_fusion.1
  903.6 12.5 %all_gather.98 = bf16[96,3072]{1,0:T(8,128)(2,1)S(1)} all-gather(bf16[24,3072]{1,0:T(8,128)(2,1)S(1)} %convert_element_type.243), channel_id=1, replica_groups=mesh['seq'=4,'shard'=8] {'seq'}, dimensions={0}, use_global_device_ids=true | all-gather | bytes 737280 | tf_op jit(solution)/shard_map/all_gather | solution.py:367
  918.2 10.4 %all_gather.100 = bf16[384,768]{1,0:T(8,128)(2,1)S(1)} all-gather(bf16[96,768]{1,0:T(8,128)(2,1)S(1)} %convert_element_type.248), channel_id=1, replica_groups=mesh['seq'=4,'shard'=8] {'seq'}, dimensions={0}, use_global_device_ids=true | all-gather | bytes 737280 | tf_op jit(solution)/shard_map/all_gather | solution.py:373
  929.7 11.9 %reduce-scatter.5.cloned.1.call-done = f32[24,2304]{1,0:T(8,128)} async-done(((f32[768,2304]{1,0:T(8,128)}), f32[24,2304]{1,0:T(8,128)}) %reduce-scatter.5.cloned.1.call-update) | async-done | bytes 221200 | tf_op jit(solution)/shard_map/reduce_scatter | solution.py:316
  942.5 10.3 %all_gather.91 = bf16[96,2304]{1,0:T(8,128)(2,1)S(1)} all-gather(bf16[24,2304]{1,0:T(8,128)(2,1)S(1)} %convert_element_type.226), channel_id=1, replica_groups=mesh['seq'=4,'shard'=8] {'seq'}, dimensions={0}, use_global_device_ids=true | all-gather | bytes 552960 | tf_op jit(solution)/shard_map/all_gather | solution.py:346
  (393 shorter events, 378.9 us)
Async XLA Ops:
  7.2 47.3 %all-gather.6.cloned.1.call-start = ((), (), s32[]{:S(2)}) async-start(), calls=%async_computation.8 | async-start | bytes 3981312 | tf_op jit(solution)/shard_map/all_gather | solution.py:172
  7.9 299.0 %all-gather.8.cloned.1.call-start = ((), (), s32[]{:S(2)}) async-start(), calls=%async_computation.9 | async-start | bytes 1327104 | tf_op jit(solution)/shard_map/all_gather | solution.py:175
  8.7 304.4 %all-gather.10.cloned.1.call-start = ((), (), s32[]{:S(2)}) async-start(), calls=%async_computation.10 | async-start | bytes 5308416 | tf_op jit(solution)/shard_map/all_gather | solution.py:179
  93.3 5.7 copy-start.36
  93.3 58.8 %all-to-all-start = ((bf16[2,512,3,4,192]{1,0,4,2,3:T(2,128)(2,1)}), bf16[2,512,3,4,192]{1,0,4,2,3:T(2,128)(2,1)}, u32[]{:S(2)}, u32[]{:S(2)}) async-start(bf16[2,512,3,4,192]{1,0,4,2,3:T(2,128)(2,1)} %copy.155), calls=%async_computation | async-start | bytes 9437184 | tf_op jit(solution)/shard_map/all_to_all | solution.py:210
  98.4 227.2 %all-gather.12.cloned.1.call-start = ((), (), s32[]{:S(2)}) async-start(), calls=%async_computation.11 | async-start | bytes 5308416 | tf_op jit(solution)/shard_map/all_gather | solution.py:181
  208.2 7.7 copy-start.4
  208.3 7.7 copy-start.7
  208.3 7.7 copy-start.11
  208.3 7.7 copy-start.22
  277.3 5.9 copy-start.35
  277.3 6.0 copy-start.34
  277.4 6.0 copy-start.33
  277.4 6.0 copy-start.37
  277.4 18.7 %copy-start.32 = (bf16[768]{0:T(1024)(128)(2,1)S(1)}, bf16[768]{0:T(1024)(128)(2,1)}, u32[]{:S(2)}) copy-start(bf16[768]{0:T(1024)(128)(2,1)} %get-tuple-element.577) | copy-start | bytes 4612
  277.4 18.7 %copy-start.31 = (bf16[768]{0:T(1024)(128)(2,1)S(1)}, bf16[768]{0:T(1024)(128)(2,1)}, u32[]{:S(2)}) copy-start(bf16[768]{0:T(1024)(128)(2,1)} %get-tuple-element.579) | copy-start | bytes 4612
  278.7 20.1 %copy-start.30 = (bf16[768]{0:T(1024)(128)(2,1)S(1)}, bf16[768]{0:T(1024)(128)(2,1)}, u32[]{:S(2)}) copy-start(bf16[768]{0:T(1024)(128)(2,1)} %get-tuple-element.578) | copy-start | bytes 4612
  278.7 23.6 %all-to-all-start.1 = ((bf16[4,2,512,1,192]{2,4,1,3,0:T(8,128)(2,1)}), bf16[4,2,512,1,192]{2,4,1,3,0:T(8,128)(2,1)}, u32[]{:S(2)}, u32[]{:S(2)}) async-start(bf16[4,2,512,1,192]{2,4,1,3,0:T(8,128)(2,1)} %pad_maximum_fusion), calls=%async_computation.1 | async-start | bytes 3145728 | tf_op jit(solution)/shard_map/all_to_all | solution.py:228
  283.2 540.1 %reduce-scatter.7.cloned.1.call-start = ((), (), s32[]{:S(2)}) async-start(), calls=%async_computation.13 | async-start | bytes 2433024 | tf_op jit(solution)/shard_map/reduce_scatter | solution.py:319
  338.1 16.6 %slice-start = ((s8[4718592]{0:T(1024)(128)(4,1)}), s8[4194304]{0:T(1024)(128)(4,1)S(1)}, s32[]{:S(2)}) async-start(s8[4718592]{0:T(1024)(128)(4,1)} %bitcast.351), calls=%async_computation.16 | async-start | bytes 8388608
  341.0 13.7 %copy-start.15 = (f32[1024,768]{1,0:T(8,128)}, f32[1024,768]{1,0:T(8,128)S(1)}, u32[]{:S(2)}) copy-start(f32[1024,768]{1,0:T(8,128)S(1)} %get-tuple-element.590) | copy-start | bytes 9437188
  341.0 13.7 %copy-start.10 = (f32[1024,768]{1,0:T(8,128)S(1)}, f32[1024,768]{1,0:T(8,128)}, u32[]{:S(2)}) copy-start(f32[1024,768]{1,0:T(8,128)} %copy-done.9) | copy-start | bytes 9437188
  341.0 13.7 %slice-start.1 = ((s8[4718592]{0:T(1024)(128)(4,1)}), s8[524288]{0:T(1024)(128)(4,1)S(1)}, s32[]{:S(2)}) async-start(s8[4718592]{0:T(1024)(128)(4,1)} %bitcast.351), calls=%async_computation.17 | async-start | bytes 1048576
  354.7 6.6 copy-start.14
  366.3 536.2 %reduce-scatter.9.cloned.1.call-start = ((), (), s32[]{:S(2)}) async-start(), calls=%async_computation.14 | async-start | bytes 9732096 | tf_op jit(solution)/shard_map/reduce_scatter | solution.py:323
  391.0 23.1 %all-to-all-start.2 = ((bf16[2,512,4,192]{1,0,3,2:T(2,128)(2,1)}), bf16[2,512,4,192]{1,0,3,2:T(2,128)(2,1)}, u32[]{:S(2)}, u32[]{:S(2)}) async-start(bf16[2,512,4,192]{1,0,3,2:T(2,128)(2,1)} %reshape.425), calls=%async_computation.2 | async-start | bytes 3145728 | tf_op jit(solution)/shard_map/all_to_all | solution.py:266
  395.3 521.8 %reduce-scatter.11.cloned.1.call-start = ((), (), s32[]{:S(2)}) async-start(), calls=%async_computation.15 | async-start | bytes 9732096 | tf_op jit(solution)/shard_map/reduce_scatter | solution.py:325
  408.5 533.0 %reduce-scatter.5.cloned.1.call-start = ((), (), s32[]{:S(2)}) async-start(), calls=%async_computation.12 | async-start | bytes 7299072 | tf_op jit(solution)/shard_map/reduce_scatter | solution.py:316
  422.7 4.5 copy-start
  432.2 11.6 %copy-start.1 = (f32[3,512,2048]{2,1,0:T(8,128)S(1)}, f32[3,512,2048]{2,1,0:T(8,128)}, u32[]{:S(2)}) copy-start(f32[3,512,2048]{2,1,0:T(8,128)} %copy-done) | copy-start | bytes 37748740 | tf_op jit(solution)/shard_map/while
  449.6 4.5 copy-start
  459.0 12.0 %copy-start.1 = (f32[3,512,2048]{2,1,0:T(8,128)S(1)}, f32[3,512,2048]{2,1,0:T(8,128)}, u32[]{:S(2)}) copy-start(f32[3,512,2048]{2,1,0:T(8,128)} %copy-done) | copy-start | bytes 37748740 | tf_op jit(solution)/shard_map/while
  478.0 4.8 copy-start
  487.8 12.7 %copy-start.1 = (f32[3,512,2048]{2,1,0:T(8,128)S(1)}, f32[3,512,2048]{2,1,0:T(8,128)}, u32[]{:S(2)}) copy-start(f32[3,512,2048]{2,1,0:T(8,128)} %copy-done) | copy-start | bytes 37748740 | tf_op jit(solution)/shard_map/while
  507.6 4.7 copy-start
  517.2 12.0 %copy-start.1 = (f32[3,512,2048]{2,1,0:T(8,128)S(1)}, f32[3,512,2048]{2,1,0:T(8,128)}, u32[]{:S(2)}) copy-start(f32[3,512,2048]{2,1,0:T(8,128)} %copy-done) | copy-start | bytes 37748740 | tf_op jit(solution)/shard_map/while
  540.9 6.4 copy-start.2
  552.3 10.9 %copy-start.3 = (f32[3,512,2048]{2,1,0:T(8,128)S(1)}, f32[3,512,2048]{2,1,0:T(8,128)}, u32[]{:S(2)}) copy-start(f32[3,512,2048]{2,1,0:T(8,128)} %copy-done.2) | copy-start | bytes 37748740 | tf_op jit(solution)/shard_map/while
  570.9 6.4 copy-start.2
  582.3 10.7 %copy-start.3 = (f32[3,512,2048]{2,1,0:T(8,128)S(1)}, f32[3,512,2048]{2,1,0:T(8,128)}, u32[]{:S(2)}) copy-start(f32[3,512,2048]{2,1,0:T(8,128)} %copy-done.2) | copy-start | bytes 37748740 | tf_op jit(solution)/shard_map/while
  601.3 6.4 copy-start.2
  612.6 11.2 %copy-start.3 = (f32[3,512,2048]{2,1,0:T(8,128)S(1)}, f32[3,512,2048]{2,1,0:T(8,128)}, u32[]{:S(2)}) copy-start(f32[3,512,2048]{2,1,0:T(8,128)} %copy-done.2) | copy-start | bytes 37748740 | tf_op jit(solution)/shard_map/while
  632.3 6.4 copy-start.2
  643.7 11.3 %copy-start.3 = (f32[3,512,2048]{2,1,0:T(8,128)S(1)}, f32[3,512,2048]{2,1,0:T(8,128)}, u32[]{:S(2)}) copy-start(f32[3,512,2048]{2,1,0:T(8,128)} %copy-done.2) | copy-start | bytes 37748740 | tf_op jit(solution)/shard_map/while
  663.1 7.0 copy-start.18
  807.7 4.0 copy-start.39
  811.7 4.2 copy-start.13
  819.5 74.6 %copy-start.20 = (f32[1024,768]{1,0:T(8,128)S(1)}, f32[1024,768]{1,0:T(8,128)}, u32[]{:S(2)}) copy-start(f32[1024,768]{1,0:T(8,128)} %copy-done.19) | copy-start | bytes 9437188
  (18 other events, 44.7 us)
Sparse Core Ops, SparseCore 0:
  9.7 44.8 all-gather.5
  56.2 21.5 all-gather.7
  79.4 51.4 all-gather.9
  132.4 50.5 all-gather.11
  366.5 97.0 reduce-scatter.6
  470.3 134.5 reduce-scatter.8
  610.8 159.8 reduce-scatter.10
  819.6 121.8 reduce-scatter.4
